TPU v7x, 512 devices: a whole 4x8x8 slice. The times are simulated.
512 devices in a mesh: head: 8 (over y_hi, core), ctx: 64 (over x, y_lo, z).
Axes of the slice: x: 4, y: 8 (y_hi: 4, y_lo: 2; y = y_hi * 2 + y_lo), z: 8, core: 2. Of those that a mesh axis runs over, the one named last changes fastest.
Arguments:
- queries: bfloat16 [65536, 4096], P(('ctx', 'head')), may hold values from -8 to 8
- saved_key_rows: bfloat16 [65536, 1024], P(('ctx', 'head')), may hold values from -8 to 8
- saved_value_rows: bfloat16 [65536, 1024], P(('ctx', 'head')), may hold values from -6 to 6
- saved_output: bfloat16 [65536, 4096], P(('ctx', 'head')), may hold values from -1.5 to 1.5
- output_gradient: bfloat16 [65536, 4096], P(('ctx', 'head')), may hold values from -6 to 6
- stripe_order: int32 [64, 1024], P('ctx'), may hold values from 0 to 1023, each once within a row
Outputs:
- query_gradient: bfloat16 [65536, 4096], P(('ctx', 'head'))
- key_grad: bfloat16 [65536, 1024], P(('ctx', 'head'))
- value_grad: bfloat16 [65536, 1024], P(('ctx', 'head'))
Inputs may be any that keep to these rules, and one draw needn't show every extreme that they name: Each row of stripe_order holds every number from 0 to 1023 once.
All inputs are finite; a program needn't handle non-finite values.
Results may differ from a plain program's by a relative error of at most 0.0049.
Values may be sent and summed in bfloat16 or wider, within the bound.
A program may use at most 64 MiB of HBM per device.

v0:
```python
import math

import jax
import jax.numpy as jnp
from jax import lax
from jax.sharding import PartitionSpec as P

HEAD_SIZE = 128


def shifted(x, axis, by):
    peers = lax.axis_size(axis)
    pairs = [(i, i + by) for i in range(peers) if 0 <= i + by < peers]
    return lax.ppermute(x, axis, pairs)


def row_sums(output_part, grad_part):
    rows, width = output_part.shape
    product = output_part.astype(jnp.float32) * grad_part.astype(jnp.float32)
    return jnp.sum(product.reshape(rows, width // HEAD_SIZE, HEAD_SIZE), axis=2)


def body(queries, saved_key_rows, saved_value_rows, saved_output, output_gradient, stripe_order):
    query_heads, key_heads, value_heads, output_heads, grad_heads = (
        lax.all_to_all(queries, "head", split_axis=1, concat_axis=0, tiled=True),
        lax.all_to_all(saved_key_rows, "head", split_axis=1, concat_axis=0, tiled=True),
        lax.all_to_all(saved_value_rows, "head", split_axis=1, concat_axis=0, tiled=True),
        lax.all_to_all(saved_output, "head", split_axis=1, concat_axis=0, tiled=True),
        lax.all_to_all(output_gradient, "head", split_axis=1, concat_axis=0, tiled=True),
    )
    delta_rows = row_sums(output_heads, grad_heads)
    block_rows = query_heads.shape[0]
    tail_rows = block_rows // 4
    order_row = stripe_order[0]
    inverse = (
        jnp.zeros((block_rows,), jnp.int32)
        .at[order_row]
        .set(jnp.arange(block_rows, dtype=jnp.int32))
    )
    tail_index = inverse[block_rows - tail_rows :]
    tail_keys = jnp.take(key_heads, tail_index, axis=0)
    tail_values = jnp.take(value_heads, tail_index, axis=0)
    prev_keys, prev_values = shifted((tail_keys, tail_values), "ctx", 1)
    keys_all = jnp.concatenate([key_heads, prev_keys], axis=0)
    values_all = jnp.concatenate([value_heads, prev_values], axis=0)
    query_count = query_heads.shape[1] // HEAD_SIZE
    score_scale = 1.0 / math.sqrt(HEAD_SIZE)
    block_index = lax.axis_index("ctx")
    own_part = order_row[None, :] <= order_row[:, None]
    prev_part = jnp.broadcast_to(block_index > 0, (block_rows, tail_rows))
    visible = jnp.concatenate([own_part, prev_part], axis=1)

    def per_head(head_index, carry):
        key_acc, value_acc, query_buf = carry
        query_one = lax.dynamic_slice_in_dim(query_heads, head_index * HEAD_SIZE, HEAD_SIZE, 1)
        grad_one = lax.dynamic_slice_in_dim(grad_heads, head_index * HEAD_SIZE, HEAD_SIZE, 1)
        delta_one = lax.dynamic_slice_in_dim(delta_rows, head_index, 1, 1)
        scores = (
            lax.dot_general(
                query_one, keys_all, (((1,), (1,)), ((), ())), preferred_element_type=jnp.float32
            )
            * score_scale
        )
        scores = jnp.where(visible, scores, -1e30)
        row_top = jnp.max(scores, axis=1, keepdims=True)
        expo = jnp.where(visible, jnp.exp(scores - row_top), 0.0)
        probs = expo / jnp.sum(expo, axis=1, keepdims=True)
        probs_b = probs.astype(jnp.bfloat16)
        dprob = lax.dot_general(
            grad_one, values_all, (((1,), (1,)), ((), ())), preferred_element_type=jnp.float32
        )
        dscore = (probs * (dprob - delta_one)).astype(jnp.bfloat16)
        query_one_grad = (
            jnp.dot(dscore, keys_all, preferred_element_type=jnp.float32) * score_scale
        ).astype(jnp.bfloat16)
        key_one_grad = (
            lax.dot_general(
                dscore, query_one, (((0,), (0,)), ((), ())), preferred_element_type=jnp.float32
            )
            * score_scale
        )
        value_one_grad = lax.dot_general(
            probs_b, grad_one, (((0,), (0,)), ((), ())), preferred_element_type=jnp.float32
        )
        key_acc = key_acc + key_one_grad
        value_acc = value_acc + value_one_grad
        query_buf = lax.dynamic_update_slice_in_dim(
            query_buf, query_one_grad, head_index * HEAD_SIZE, 1
        )
        return (key_acc, value_acc, query_buf)

    start_keys = jnp.zeros(keys_all.shape, jnp.float32)
    start_values = jnp.zeros(values_all.shape, jnp.float32)
    start_query = jnp.zeros(query_heads.shape, jnp.bfloat16)
    key_acc, value_acc, query_buf = lax.fori_loop(
        0, query_count, per_head, (start_keys, start_values, start_query)
    )
    back_keys, back_values = shifted((key_acc[block_rows:], value_acc[block_rows:]), "ctx", -1)
    key_gradient_total = key_acc[:block_rows].at[tail_index].add(back_keys).astype(jnp.bfloat16)
    value_gradient_total = (
        value_acc[:block_rows].at[tail_index].add(back_values).astype(jnp.bfloat16)
    )
    query_gradient, key_grad, value_grad = (
        lax.all_to_all(query_buf, "head", split_axis=0, concat_axis=1, tiled=True),
        lax.all_to_all(key_gradient_total, "head", split_axis=0, concat_axis=1, tiled=True),
        lax.all_to_all(value_gradient_total, "head", split_axis=0, concat_axis=1, tiled=True),
    )
    return (query_gradient, key_grad, value_grad)


def solution(mesh):
    in_specs = (
        P(("ctx", "head"), None),
        P(("ctx", "head"), None),
        P(("ctx", "head"), None),
        P(("ctx", "head"), None),
        P(("ctx", "head"), None),
        P("ctx", None),
    )
    out_specs = (P(("ctx", "head"), None), P(("ctx", "head"), None), P(("ctx", "head"), None))
    return jax.shard_map(body, mesh=mesh, in_specs=in_specs, out_specs=out_specs, check_vma=False)
```

profile of v0, /device:TPU:8, one launch (start us, length us, event | category | flops | bytes accessed | tf_op | source)
XLA Modules:
  0.0 304.5 jit_solution(6210915375914858110)
XLA Ops:
  2.3 6.2 %all-to-all-start.1 = ((bf16[128,8,128]{2,0,1:T(8,128)(2,1)}), bf16[128,8,128]{2,0,1:T(8,128)(2,1)S(1)}, u32[]{:S(2)}, u32[]{:S(2)}) async-start(bf16[128,8,128]{2,0,1:T(8,128)(2,1)} %copy_bitcast_fusion.4), calls=%async_computation.1 | async-start | bytes 524288 | tf_op jit(solution)/shard_map/all_to_all | solution.py:26
  10.2 11.1 %all-to-all-done.1 = bf16[128,8,128]{2,0,1:T(8,128)(2,1)S(1)} async-done(((bf16[128,8,128]{2,0,1:T(8,128)(2,1)}), bf16[128,8,128]{2,0,1:T(8,128)(2,1)S(1)}, u32[]{:S(2)}, u32[]{:S(2)}) %all-to-all-start.1) | async-done | bytes 262176 | tf_op jit(solution)/shard_map/all_to_all | solution.py:26
  21.3 3.4 %all-to-all-start.3 = ((bf16[128,8,128]{2,0,1:T(8,128)(2,1)}), bf16[128,8,128]{2,0,1:T(8,128)(2,1)S(1)}, u32[]{:S(2)}, u32[]{:S(2)}) async-start(bf16[128,8,128]{2,0,1:T(8,128)(2,1)} %copy_bitcast_fusion.3), calls=%async_computation.3 | async-start | bytes 524288 | tf_op jit(solution)/shard_map/all_to_all | solution.py:27
  24.7 2.3 copy.54
  27.0 10.4 %all-to-all-done.3 = bf16[128,8,128]{2,0,1:T(8,128)(2,1)S(1)} async-done(((bf16[128,8,128]{2,0,1:T(8,128)(2,1)}), bf16[128,8,128]{2,0,1:T(8,128)(2,1)S(1)}, u32[]{:S(2)}, u32[]{:S(2)}) %all-to-all-start.3) | async-done | bytes 262176 | tf_op jit(solution)/shard_map/all_to_all | solution.py:27
  37.4 3.7 %all-to-all-start.2 = ((bf16[128,8,512]{2,0,1:T(8,128)(2,1)}), bf16[128,8,512]{2,0,1:T(8,128)(2,1)S(1)}, u32[]{:S(2)}, u32[]{:S(2)}) async-start(bf16[128,8,512]{2,0,1:T(8,128)(2,1)} %bitcast.57), calls=%async_computation.2 | async-start | bytes 2097152 | tf_op jit(solution)/shard_map/all_to_all | solution.py:29
  42.2 27.8 %all-to-all-done.2 = bf16[128,8,512]{2,0,1:T(8,128)(2,1)S(1)} async-done(((bf16[128,8,512]{2,0,1:T(8,128)(2,1)}), bf16[128,8,512]{2,0,1:T(8,128)(2,1)S(1)}, u32[]{:S(2)}, u32[]{:S(2)}) %all-to-all-start.2) | async-done | bytes 1048608 | tf_op jit(solution)/shard_map/all_to_all | solution.py:29
  70.0 3.6 %all-to-all-start.4 = ((bf16[128,8,512]{2,0,1:T(8,128)(2,1)}), bf16[128,8,512]{2,0,1:T(8,128)(2,1)S(1)}, u32[]{:S(2)}, u32[]{:S(2)}) async-start(bf16[128,8,512]{2,0,1:T(8,128)(2,1)} %bitcast.56), calls=%async_computation.4 | async-start | bytes 2097152 | tf_op jit(solution)/shard_map/all_to_all | solution.py:28
  73.6 2.3 copy.55
  75.9 4.3 %scatter_custom_fusion = s32[1024]{0:T(1024)S(1)} fusion(s32[1024]{0:T(1024)S(1)} %bitcast.85, s32[1024]{0:T(1024)S(1)} %iota.3, s32[]{:T(128)} %constant.81.clone.1), kind=kCustom, calls=%fused_computation.41 | custom fusion | bytes 4100 | tf_op jit(solution)/shard_map/scatter | solution.py:38
  80.2 22.7 %all-to-all-done.4 = bf16[128,8,512]{2,0,1:T(8,128)(2,1)S(1)} async-done(((bf16[128,8,512]{2,0,1:T(8,128)(2,1)}), bf16[128,8,512]{2,0,1:T(8,128)(2,1)S(1)}, u32[]{:S(2)}, u32[]{:S(2)}) %all-to-all-start.4) | async-done | bytes 1048608 | tf_op jit(solution)/shard_map/all_to_all | solution.py:28
  102.9 4.2 %all-to-all-start = ((bf16[128,8,512]{2,0,1:T(8,128)(2,1)}), bf16[128,8,512]{2,0,1:T(8,128)(2,1)}, u32[]{:S(2)}, u32[]{:S(2)}) async-start(bf16[128,8,512]{2,0,1:T(8,128)(2,1)} %bitcast.58), calls=%async_computation | async-start | bytes 2097152 | tf_op jit(solution)/shard_map/all_to_all | solution.py:25
  110.2 3.8 %collective-permute-start = (bf16[256,128]{1,0:T(8,128)(2,1)}, bf16[256,128]{1,0:T(8,128)(2,1)}, u32[]{:S(2)}, u32[]{:S(2)}) collective-permute-start(bf16[256,128]{1,0:T(8,128)(2,1)} %get-tuple-element.257), channel_id=1, source_target_pairs={{0,1},{1,2},{2,3},{3,4},{4,5},{5,6},{6,7},{7,8},{8,9},{9,10},{10,1... | collective-permute-start | bytes 196616 | tf_op jit(solution)/shard_map/ppermute | solution.py:14
  117.5 4.5 %collective-permute-start.1 = (bf16[256,128]{1,0:T(8,128)(2,1)}, bf16[256,128]{1,0:T(8,128)(2,1)S(1)}, u32[]{:S(2)}, u32[]{:S(2)}) collective-permute-start(bf16[256,128]{1,0:T(8,128)(2,1)} %get-tuple-element.256), channel_id=1, source_target_pairs={{0,1},{1,2},{2,3},{3,4},{4,5},{5,6},{6,7},{7,8},{8,9},{9,10},{10,1... | collective-permute-start | bytes 196616 | tf_op jit(solution)/shard_map/ppermute | solution.py:14
  122.0 18.4 %collective-permute-done = bf16[256,128]{1,0:T(8,128)(2,1)} collective-permute-done((bf16[256,128]{1,0:T(8,128)(2,1)}, bf16[256,128]{1,0:T(8,128)(2,1)}, u32[]{:S(2)}, u32[]{:S(2)}) %collective-permute-start) | collective-permute-done | bytes 65568 | tf_op jit(solution)/shard_map/ppermute | solution.py:14
  145.6 2.9 mul.45
  148.5 3.6 %reduce_sum.22 = f32[1024,4]{1,0:T(8,128)} reduce(f32[1024,4,128]{2,1,0:T(4,128)} %mul.45, f32[]{:T(128)} %constant.82.clone.1), dimensions={2}, to_apply=%region_0.0 | reduce | flops 520192 | bytes 2113540 | tf_op jit(solution)/shard_map/reduce_sum | solution.py:20
  154.4 62.1 %while.18 = (s32[]{:T(128)}, f32[1280,128]{1,0:T(8,128)S(1)}, f32[1280,128]{1,0:T(8,128)}, bf16[1024,512]{1,0:T(8,128)(2,1)}, bf16[1024,512]{1,0:T(8,128)(2,1)},...) while((s32[]{:T(128)}, f32[1280,128]{1,0:T(8,128)S(1)}, ...), condition=%wide.region_5.7_spmd.clone, body=%wide.region_2.6_spmd.clone.sunk | while | flops 1695840256 | bytes 111641024 | solution.py:95
  154.4 2.7 fusion.52
  158.5 1.9 fusion.54
  160.4 2.2 multiply_convert_fusion.2
  164.2 2.3 fusion.55
  166.8 2.9 fusion.56
  169.7 2.7 fusion.52
  173.8 1.9 fusion.54
  175.8 2.2 multiply_convert_fusion.2
  179.6 2.3 fusion.55
  182.2 3.1 %fusion.56 = f32[1280,128]{1,0:T(8,128)} fusion(f32[1024,1280]{1,0:T(8,128)S(1)} %copy-done.2, f32[1280,128]{1,0:T(8,128)} %get-tuple-element.339, pred[]{:T(512)S(6)} %compare.4, bf16[1024,512]{1,0:T(8,128)(2,1)} %copy-done.5, s32[]{:T(128)S(6)} %select_n.78), kind=kOutput, calls=%fused_computation.14.clone.1 | convolution fusion | flops 337182720 | bytes 6815749 | tf_op jit(solution)/shard_map/while/body/eval_jaxpr/dot_general | solution.py:82
  185.3 2.7 fusion.52
  189.4 1.9 fusion.54
  191.4 2.2 multiply_convert_fusion.2
  195.2 2.3 fusion.55
  197.8 3.1 %fusion.56 = f32[1280,128]{1,0:T(8,128)} fusion(f32[1024,1280]{1,0:T(8,128)S(1)} %copy-done.2, f32[1280,128]{1,0:T(8,128)} %get-tuple-element.339, pred[]{:T(512)S(6)} %compare.4, bf16[1024,512]{1,0:T(8,128)(2,1)} %copy-done.5, s32[]{:T(128)S(6)} %select_n.78), kind=kOutput, calls=%fused_computation.14.clone.1 | convolution fusion | flops 337182720 | bytes 6815749 | tf_op jit(solution)/shard_map/while/body/eval_jaxpr/dot_general | solution.py:82
  200.9 2.7 fusion.52
  205.0 1.9 fusion.54
  207.0 2.2 multiply_convert_fusion.2
  210.8 2.3 fusion.55
  213.4 3.1 %fusion.56 = f32[1280,128]{1,0:T(8,128)} fusion(f32[1024,1280]{1,0:T(8,128)S(1)} %copy-done.2, f32[1280,128]{1,0:T(8,128)} %get-tuple-element.339, pred[]{:T(512)S(6)} %compare.4, bf16[1024,512]{1,0:T(8,128)(2,1)} %copy-done.5, s32[]{:T(128)S(6)} %select_n.78), kind=kOutput, calls=%fused_computation.14.clone.1 | convolution fusion | flops 337182720 | bytes 6815749 | tf_op jit(solution)/shard_map/while/body/eval_jaxpr/dot_general | solution.py:82
  217.4 1.9 collective-permute-start.3
  220.4 4.1 %collective-permute-done.3 = f32[256,128]{1,0:T(8,128)S(1)} collective-permute-done((f32[256,128]{1,0:T(8,128)S(1)}, f32[256,128]{1,0:T(8,128)S(1)}, u32[]{:S(2)}, u32[]{:S(2)}) %collective-permute-start.3) | collective-permute-done | bytes 131104 | tf_op jit(solution)/shard_map/ppermute | solution.py:14
  224.6 2.3 scatter_fusion.1
  227.6 7.6 %all-to-all-start.7 = ((bf16[8,128,128]{2,1,0:T(8,128)(2,1)}), bf16[8,128,128]{2,1,0:T(8,128)(2,1)S(1)}, u32[]{:S(2)}, u32[]{:S(2)}) async-start(bf16[8,128,128]{2,1,0:T(8,128)(2,1)} %bitcast.20), calls=%async_computation.7 | async-start | bytes 524288 | tf_op jit(solution)/shard_map/all_to_all | solution.py:106
  235.1 4.2 %collective-permute-start.2 = (f32[256,128]{1,0:T(8,128)S(1)}, f32[256,128]{1,0:T(8,128)S(1)}, u32[]{:S(2)}, u32[]{:S(2)}) collective-permute-start(f32[256,128]{1,0:T(8,128)S(1)} %slice.17), channel_id=1, source_target_pairs={{1,0},{2,1},{3,2},{4,3},{5,4},{6,5},{7,6},{8,7},{9,8},{10,9},{11,1... | collective-permute-start | bytes 393224 | tf_op jit(solution)/shard_map/ppermute | solution.py:14
  239.4 5.3 %collective-permute-done.2 = f32[256,128]{1,0:T(8,128)S(1)} collective-permute-done((f32[256,128]{1,0:T(8,128)S(1)}, f32[256,128]{1,0:T(8,128)S(1)}, u32[]{:S(2)}, u32[]{:S(2)}) %collective-permute-start.2) | collective-permute-done | bytes 131104 | tf_op jit(solution)/shard_map/ppermute | solution.py:14
  244.7 2.1 scatter_fusion
  247.6 27.4 %all_to_all.146 = bf16[8,128,128]{2,1,0:T(8,128)(2,1)S(1)} all-to-all(bf16[8,128,128]{2,1,0:T(8,128)(2,1)S(1)} %bitcast.77), channel_id=1, replica_groups=mesh['head'=8,'ctx'=64] {'head'}, dimensions={0} | all-to-all | bytes 524288 | tf_op jit(solution)/shard_map/all_to_all | solution.py:105
  274.9 3.6 %all-to-all-start.5 = ((bf16[8,128,512]{2,1,0:T(8,128)(2,1)}), bf16[8,128,512]{2,1,0:T(8,128)(2,1)S(1)}, u32[]{:S(2)}, u32[]{:S(2)}) async-start(bf16[8,128,512]{2,1,0:T(8,128)(2,1)} %bitcast.14), calls=%async_computation.5 | async-start | bytes 2097152 | tf_op jit(solution)/shard_map/all_to_all | solution.py:104
  280.6 21.9 %all-to-all-done.5 = bf16[8,128,512]{2,1,0:T(8,128)(2,1)S(1)} async-done(((bf16[8,128,512]{2,1,0:T(8,128)(2,1)}), bf16[8,128,512]{2,1,0:T(8,128)(2,1)S(1)}, u32[]{:S(2)}, u32[]{:S(2)}) %all-to-all-start.5) | async-done | bytes 1048608 | tf_op jit(solution)/shard_map/all_to_all | solution.py:104
  (127 shorter events, 39.3 us)
Async XLA Ops:
  0.6 40.4 %copy-start.12 = (bf16[128,4096]{1,0:T(8,128)(2,1)S(1)}, bf16[128,4096]{1,0:T(8,128)(2,1)}, u32[]{:S(2)}) copy-start(bf16[128,4096]{1,0:T(8,128)(2,1)} %param.13) | copy-start | bytes 3145732
  2.3 19.0 %all-to-all-start.1 = ((bf16[128,8,128]{2,0,1:T(8,128)(2,1)}), bf16[128,8,128]{2,0,1:T(8,128)(2,1)S(1)}, u32[]{:S(2)}, u32[]{:S(2)}) async-start(bf16[128,8,128]{2,0,1:T(8,128)(2,1)} %copy_bitcast_fusion.4), calls=%async_computation.1 | async-start | bytes 524288 | tf_op jit(solution)/shard_map/all_to_all | solution.py:26
  21.3 16.1 %all-to-all-start.3 = ((bf16[128,8,128]{2,0,1:T(8,128)(2,1)}), bf16[128,8,128]{2,0,1:T(8,128)(2,1)S(1)}, u32[]{:S(2)}, u32[]{:S(2)}) async-start(bf16[128,8,128]{2,0,1:T(8,128)(2,1)} %copy_bitcast_fusion.3), calls=%async_computation.3 | async-start | bytes 524288 | tf_op jit(solution)/shard_map/all_to_all | solution.py:27
  37.4 71.2 %copy-start.9 = (bf16[128,8,128]{2,0,1:T(8,128)(2,1)}, bf16[128,8,128]{2,0,1:T(8,128)(2,1)S(1)}, u32[]{:S(2)}) copy-start(bf16[128,8,128]{2,0,1:T(8,128)(2,1)S(1)} %all-to-all-done.3) | copy-start | bytes 786436
  37.4 38.5 %copy-start.13 = (s32[1,1024]{1,0:T(1,128)S(1)}, s32[1,1024]{1,0:T(1,128)}, u32[]{:S(2)}) copy-start(s32[1,1024]{1,0:T(1,128)} %param.15) | copy-start | bytes 12292
  37.4 32.6 %all-to-all-start.2 = ((bf16[128,8,512]{2,0,1:T(8,128)(2,1)}), bf16[128,8,512]{2,0,1:T(8,128)(2,1)S(1)}, u32[]{:S(2)}, u32[]{:S(2)}) async-start(bf16[128,8,512]{2,0,1:T(8,128)(2,1)} %bitcast.57), calls=%async_computation.2 | async-start | bytes 2097152 | tf_op jit(solution)/shard_map/all_to_all | solution.py:29
  70.0 32.9 %all-to-all-start.4 = ((bf16[128,8,512]{2,0,1:T(8,128)(2,1)}), bf16[128,8,512]{2,0,1:T(8,128)(2,1)S(1)}, u32[]{:S(2)}, u32[]{:S(2)}) async-start(bf16[128,8,512]{2,0,1:T(8,128)(2,1)} %bitcast.56), calls=%async_computation.4 | async-start | bytes 2097152 | tf_op jit(solution)/shard_map/all_to_all | solution.py:28
  102.9 12.7 %copy-start.10 = (bf16[128,8,512]{2,0,1:T(8,128)(2,1)}, bf16[128,8,512]{2,0,1:T(8,128)(2,1)S(1)}, u32[]{:S(2)}) copy-start(bf16[128,8,512]{2,0,1:T(8,128)(2,1)S(1)} %all-to-all-done.4) | copy-start | bytes 3145732
  102.9 50.4 %all-to-all-start = ((bf16[128,8,512]{2,0,1:T(8,128)(2,1)}), bf16[128,8,512]{2,0,1:T(8,128)(2,1)}, u32[]{:S(2)}, u32[]{:S(2)}) async-start(bf16[128,8,512]{2,0,1:T(8,128)(2,1)} %bitcast.58), calls=%async_computation | async-start | bytes 2097152 | tf_op jit(solution)/shard_map/all_to_all | solution.py:25
  110.2 30.2 %collective-permute-start = (bf16[256,128]{1,0:T(8,128)(2,1)}, bf16[256,128]{1,0:T(8,128)(2,1)}, u32[]{:S(2)}, u32[]{:S(2)}) collective-permute-start(bf16[256,128]{1,0:T(8,128)(2,1)} %get-tuple-element.257), channel_id=1, source_target_pairs={{0,1},{1,2},{2,3},{3,4},{4,5},{5,6},{6,7},{7,8},{8,9},{9,10},{10,1... | collective-permute-start | bytes 196616 | tf_op jit(solution)/shard_map/ppermute | solution.py:14
  115.7 28.3 %copy-start.11 = (bf16[128,8,512]{2,0,1:T(8,128)(2,1)S(1)}, bf16[128,8,512]{2,0,1:T(8,128)(2,1)}, u32[]{:S(2)}) copy-start(bf16[128,8,512]{2,0,1:T(8,128)(2,1)} %copy-done.10) | copy-start | bytes 3145732
  117.5 24.8 %collective-permute-start.1 = (bf16[256,128]{1,0:T(8,128)(2,1)}, bf16[256,128]{1,0:T(8,128)(2,1)S(1)}, u32[]{:S(2)}, u32[]{:S(2)}) collective-permute-start(bf16[256,128]{1,0:T(8,128)(2,1)} %get-tuple-element.256), channel_id=1, source_target_pairs={{0,1},{1,2},{2,3},{3,4},{4,5},{5,6},{6,7},{7,8},{8,9},{9,10},{10,1... | collective-permute-start | bytes 196616 | tf_op jit(solution)/shard_map/ppermute | solution.py:14
  154.4 4.0 %copy-start.3 = (pred[1024,1280]{1,0:T(32,128)(4,1)}, pred[1024,1280]{1,0:T(32,128)(4,1)S(1)}, u32[]{:S(2)}) copy-start(pred[1024,1280]{1,0:T(32,128)(4,1)S(1)} %get-tuple-element.357) | copy-start | bytes 3932164 | tf_op jit(solution)/shard_map/while
  154.4 4.1 %copy-start.5 = (bf16[1024,512]{1,0:T(8,128)(2,1)}, bf16[1024,512]{1,0:T(8,128)(2,1)S(1)}, u32[]{:S(2)}) copy-start(bf16[1024,512]{1,0:T(8,128)(2,1)S(1)} %get-tuple-element.358) | copy-start | bytes 3145732 | tf_op jit(solution)/shard_map/while
  158.4 1.9 copy-start.8
  160.4 2.3 copy-start.1
  160.4 2.3 copy-start.7
  164.2 2.6 copy-start.2
  166.5 3.2 %copy-start.4 = (pred[1024,1280]{1,0:T(32,128)(4,1)S(1)}, pred[1024,1280]{1,0:T(32,128)(4,1)}, u32[]{:S(2)}) copy-start(pred[1024,1280]{1,0:T(32,128)(4,1)} %copy-done.3) | copy-start | bytes 3932164 | tf_op jit(solution)/shard_map/while
  166.5 3.2 %copy-start.6 = (bf16[1024,512]{1,0:T(8,128)(2,1)S(1)}, bf16[1024,512]{1,0:T(8,128)(2,1)}, u32[]{:S(2)}) copy-start(bf16[1024,512]{1,0:T(8,128)(2,1)} %copy-done.5) | copy-start | bytes 3145732 | tf_op jit(solution)/shard_map/while
  169.7 4.1 %copy-start.3 = (pred[1024,1280]{1,0:T(32,128)(4,1)}, pred[1024,1280]{1,0:T(32,128)(4,1)S(1)}, u32[]{:S(2)}) copy-start(pred[1024,1280]{1,0:T(32,128)(4,1)S(1)} %get-tuple-element.357) | copy-start | bytes 3932164 | tf_op jit(solution)/shard_map/while
  169.7 4.1 %copy-start.5 = (bf16[1024,512]{1,0:T(8,128)(2,1)}, bf16[1024,512]{1,0:T(8,128)(2,1)S(1)}, u32[]{:S(2)}) copy-start(bf16[1024,512]{1,0:T(8,128)(2,1)S(1)} %get-tuple-element.358) | copy-start | bytes 3145732 | tf_op jit(solution)/shard_map/while
  173.8 1.9 copy-start.8
  175.7 2.3 copy-start.1
  175.8 2.3 copy-start.7
  179.6 2.6 copy-start.2
  181.9 3.4 %copy-start.4 = (pred[1024,1280]{1,0:T(32,128)(4,1)S(1)}, pred[1024,1280]{1,0:T(32,128)(4,1)}, u32[]{:S(2)}) copy-start(pred[1024,1280]{1,0:T(32,128)(4,1)} %copy-done.3) | copy-start | bytes 3932164 | tf_op jit(solution)/shard_map/while
  181.9 3.4 %copy-start.6 = (bf16[1024,512]{1,0:T(8,128)(2,1)S(1)}, bf16[1024,512]{1,0:T(8,128)(2,1)}, u32[]{:S(2)}) copy-start(bf16[1024,512]{1,0:T(8,128)(2,1)} %copy-done.5) | copy-start | bytes 3145732 | tf_op jit(solution)/shard_map/while
  185.3 4.1 %copy-start.3 = (pred[1024,1280]{1,0:T(32,128)(4,1)}, pred[1024,1280]{1,0:T(32,128)(4,1)S(1)}, u32[]{:S(2)}) copy-start(pred[1024,1280]{1,0:T(32,128)(4,1)S(1)} %get-tuple-element.357) | copy-start | bytes 3932164 | tf_op jit(solution)/shard_map/while
  185.3 4.1 %copy-start.5 = (bf16[1024,512]{1,0:T(8,128)(2,1)}, bf16[1024,512]{1,0:T(8,128)(2,1)S(1)}, u32[]{:S(2)}) copy-start(bf16[1024,512]{1,0:T(8,128)(2,1)S(1)} %get-tuple-element.358) | copy-start | bytes 3145732 | tf_op jit(solution)/shard_map/while
  189.4 1.9 copy-start.8
  191.3 2.3 copy-start.1
  191.4 2.3 copy-start.7
  195.2 2.6 copy-start.2
  197.5 3.4 %copy-start.4 = (pred[1024,1280]{1,0:T(32,128)(4,1)S(1)}, pred[1024,1280]{1,0:T(32,128)(4,1)}, u32[]{:S(2)}) copy-start(pred[1024,1280]{1,0:T(32,128)(4,1)} %copy-done.3) | copy-start | bytes 3932164 | tf_op jit(solution)/shard_map/while
  197.5 3.4 %copy-start.6 = (bf16[1024,512]{1,0:T(8,128)(2,1)S(1)}, bf16[1024,512]{1,0:T(8,128)(2,1)}, u32[]{:S(2)}) copy-start(bf16[1024,512]{1,0:T(8,128)(2,1)} %copy-done.5) | copy-start | bytes 3145732 | tf_op jit(solution)/shard_map/while
  200.9 4.1 %copy-start.3 = (pred[1024,1280]{1,0:T(32,128)(4,1)}, pred[1024,1280]{1,0:T(32,128)(4,1)S(1)}, u32[]{:S(2)}) copy-start(pred[1024,1280]{1,0:T(32,128)(4,1)S(1)} %get-tuple-element.357) | copy-start | bytes 3932164 | tf_op jit(solution)/shard_map/while
  200.9 4.1 %copy-start.5 = (bf16[1024,512]{1,0:T(8,128)(2,1)}, bf16[1024,512]{1,0:T(8,128)(2,1)S(1)}, u32[]{:S(2)}) copy-start(bf16[1024,512]{1,0:T(8,128)(2,1)S(1)} %get-tuple-element.358) | copy-start | bytes 3145732 | tf_op jit(solution)/shard_map/while
  206.9 2.3 copy-start.1
  207.0 2.3 copy-start.7
  210.8 2.6 copy-start.2
  213.1 3.4 %copy-start.4 = (pred[1024,1280]{1,0:T(32,128)(4,1)S(1)}, pred[1024,1280]{1,0:T(32,128)(4,1)}, u32[]{:S(2)}) copy-start(pred[1024,1280]{1,0:T(32,128)(4,1)} %copy-done.3) | copy-start | bytes 3932164 | tf_op jit(solution)/shard_map/while
  213.1 3.4 %copy-start.6 = (bf16[1024,512]{1,0:T(8,128)(2,1)S(1)}, bf16[1024,512]{1,0:T(8,128)(2,1)}, u32[]{:S(2)}) copy-start(bf16[1024,512]{1,0:T(8,128)(2,1)} %copy-done.5) | copy-start | bytes 3145732 | tf_op jit(solution)/shard_map/while
  216.5 28.2 %copy-start.15 = (s32[256]{0:T(256)S(1)}, s32[256]{0:T(256)}, u32[]{:S(2)}) copy-start(s32[256]{0:T(256)} %copy-done.14) | copy-start | bytes 3076
  217.4 7.1 %collective-permute-start.3 = (f32[256,128]{1,0:T(8,128)S(1)}, f32[256,128]{1,0:T(8,128)S(1)}, u32[]{:S(2)}, u32[]{:S(2)}) collective-permute-start(f32[256,128]{1,0:T(8,128)S(1)} %slice.19), channel_id=1, source_target_pairs={{1,0},{2,1},{3,2},{4,3},{5,4},{6,5},{7,6},{8,7},{9,8},{10,9},{11,1... | collective-permute-start | bytes 393224 | tf_op jit(solution)/shard_map/ppermute | solution.py:14
  227.6 20.0 %all-to-all-start.7 = ((bf16[8,128,128]{2,1,0:T(8,128)(2,1)}), bf16[8,128,128]{2,1,0:T(8,128)(2,1)S(1)}, u32[]{:S(2)}, u32[]{:S(2)}) async-start(bf16[8,128,128]{2,1,0:T(8,128)(2,1)} %bitcast.20), calls=%async_computation.7 | async-start | bytes 524288 | tf_op jit(solution)/shard_map/all_to_all | solution.py:106
  235.1 9.6 %collective-permute-start.2 = (f32[256,128]{1,0:T(8,128)S(1)}, f32[256,128]{1,0:T(8,128)S(1)}, u32[]{:S(2)}, u32[]{:S(2)}) collective-permute-start(f32[256,128]{1,0:T(8,128)S(1)} %slice.17), channel_id=1, source_target_pairs={{1,0},{2,1},{3,2},{4,3},{5,4},{6,5},{7,6},{8,7},{9,8},{10,9},{11,1... | collective-permute-start | bytes 393224 | tf_op jit(solution)/shard_map/ppermute | solution.py:14
  274.9 27.6 %all-to-all-start.5 = ((bf16[8,128,512]{2,1,0:T(8,128)(2,1)}), bf16[8,128,512]{2,1,0:T(8,128)(2,1)S(1)}, u32[]{:S(2)}, u32[]{:S(2)}) async-start(bf16[8,128,512]{2,1,0:T(8,128)(2,1)} %bitcast.14), calls=%async_computation.5 | async-start | bytes 2097152 | tf_op jit(solution)/shard_map/all_to_all | solution.py:104
  (3 other events, 3.4 us)
where the time goes:
time: 306 us; the launch traced here: 305 us
  waiting for transfers between devices  123 us (40%)
  matrix products  46.9 us (15%)
  starting transfers between devices  46.7 us (15%)
  local copies, waits for them, and re-layouts  30.4 us (10%)
  other arithmetic  29.1 us (10%)
  blocking collectives  27.4 us (9%)
    ppermute x4, waiting for transfers between devices, shifted(): return lax.ppermute(x, axis, pairs)  28.2 us
    all_to_all x1, waiting for transfers between devices, body(): lax.all_to_all(output_gradient, 'head', split_axis=1, concat_axis=0, tile...  27.8 us
    all_to_all x1, blocking collectives, body(): lax.all_to_all(key_gradient_total, 'head', split_axis=0, concat_axis=1, t...  27.4 us
    all_to_all x1, waiting for transfers between devices, body(): lax.all_to_all(saved_output, 'head', split_axis=1, concat_axis=0, tiled=T...  22.7 us
    all_to_all x1, waiting for transfers between devices, body(): lax.all_to_all(query_buf, 'head', split_axis=0, concat_axis=1, tiled=True)  21.9 us
    ppermute x4, starting transfers between devices, shifted(): return lax.ppermute(x, axis, pairs)  14.4 us
    dot_general x4, matrix products, per_head(): lax.dot_general(probs_b, grad_one, (((0,), (0,)), ((), ())), preferred_el...  12.2 us
    all_to_all x1, waiting for transfers between devices, body(): lax.all_to_all(saved_key_rows, 'head', split_axis=1, concat_axis=0, tiled...  11.1 us
  transfers between devices with their start and end apart: 11, of which 10 were waited for; matrix products, arithmetic and copies ran while one was open for 12% of the time, Pallas kernels for 0%

commit v1 on v0

v1 whole, which is shorter than its diff:
```python
import math

import jax
import jax.numpy as jnp
from jax import lax
from jax.experimental import pallas as pl
from jax.experimental.pallas import tpu as pltpu
from jax.sharding import PartitionSpec as P

HEAD = 128
HEADS = 4
GROUP = 4
ROWS = 128
CHIP_ROWS = 256
BLOCK = 1024
TAIL = 256
KEYS = BLOCK + TAIL
SCALE = 1.0 / math.sqrt(HEAD)
EXP_SCALE = SCALE * math.log2(math.e)
MASKED = -1e30
MESH = pl.DeviceIdType.MESH
F32 = jnp.float32
BF16 = jnp.bfloat16
NN = (((1,), (0,)), ((), ()))
NT = (((1,), (1,)), ((), ()))
TN = (((0,), (0,)), ((), ()))


def dot(a, b, dims=NN):
    return lax.dot_general(a, b, dims, preferred_element_type=F32)


def tile(start, size):
    return pl.ds(pl.multiple_of(start, size), size)


def kernel(
    q_in, k_in, v_in, o_in, g_in, order,
    dq_out, dk_out, dv_out,
    q, g, o, kv, bias, take, give, delta, probs, dscore, acc, dq,
    tail_send, back_send, back_recv, hop_send, hop_recv, out_stage,
    load_sem, own_sem, pair_send, pair_recv,
    first_send, first_recv, sib_send, sib_recv, fwd_send, fwd_recv,
    tail_ssem, tail_rsem, back_ssem, back_rsem, hop_ssem, hop_rsem,
    dq_own, dq_ssem, dq_rsem, kv_own, kv_ssem, kv_rsem,
):
    h = lax.axis_index("head")
    block = lax.axis_index("ctx")
    core = h % 2
    chip = h // 2
    right, left, far = (chip + 1) % 4, (chip + 3) % 4, (chip + 2) % 4
    sib = chip * 2 + 1 - core
    after, before = (block + 1) % 64, (block + 63) % 64
    lo, hi = pl.ds(0, HEAD), pl.ds(HEAD, HEAD)
    right_dev, left_dev, sib_dev = {"head": right * 2 + core}, {"head": left * 2 + core}, {"head": sib}
    after_dev, before_dev = {"ctx": after}, {"ctx": before}
    own_rows = tile(core * ROWS, ROWS)
    sib_rows = tile((1 - core) * ROWS, ROWS)
    wide = GROUP * HEADS * HEAD
    own_cols = tile(core * wide, wide)
    sib_cols = tile((1 - core) * wide, wide)

    def remote(src, dst, ssem, rsem, dev):
        return pltpu.make_async_remote_copy(
            src_ref=src, dst_ref=dst, send_sem=ssem, recv_sem=rsem, device_id=dev, device_id_type=MESH
        )

    def landed(ref, sem):
        pltpu.make_async_copy(ref, ref, sem).wait()

    def chip_rows(c):
        return tile(c * CHIP_ROWS, CHIP_ROWS)

    def block_rows(c, k):
        return tile((c * 2 + k) * ROWS, ROWS)

    def head_cols(k, j):
        return tile((k * HEADS + j) * HEAD, HEAD)

    pairs = ((q_in, q), (g_in, g), (o_in, o))
    loads = [
        pltpu.make_async_copy(src.at[:, own_cols], dst.at[own_rows, :], load_sem.at[i])
        for i, (src, dst) in enumerate(pairs)
    ]
    for c in loads:
        c.start()

    barrier = pltpu.get_barrier_semaphore()
    for dev in (
        {"head": right * 2}, {"head": right * 2 + 1}, {"head": left * 2}, {"head": left * 2 + 1},
        sib_dev, after_dev, before_dev,
    ):
        pl.semaphore_signal(barrier, inc=1, device_id=dev, device_id_type=MESH)
    pl.semaphore_wait(barrier, 7)

    def first_copies(j):
        out = []
        for n, (src, part, to) in enumerate(
            ((k_in, lo, right), (v_in, hi, left), (k_in, lo, left), (v_in, hi, right))
        ):
            for k in range(2):
                out.append(
                    remote(
                        src.at[:, head_cols(k, j)], kv.at[j, block_rows(chip, core), part],
                        first_send.at[j, 2 * n + k], first_recv.at[j, n], {"head": to * 2 + k},
                    )
                )
        return out

    def sib_copies(j):
        return [
            remote(
                src.at[:, head_cols(1 - core, j)], kv.at[j, block_rows(chip, core), part],
                sib_send.at[j, n], sib_recv.at[j], sib_dev,
            )
            for n, (src, part) in enumerate(((k_in, lo), (v_in, hi)))
        ]

    def own_copies(j):
        return [
            pltpu.make_async_copy(
                src.at[:, head_cols(core, j)], kv.at[j, block_rows(chip, core), part], own_sem.at[j, n]
            )
            for n, (src, part) in enumerate(((k_in, lo), (v_in, hi)))
        ]

    def start_first(j):
        for c in first_copies(j) + sib_copies(j) + own_copies(j):
            c.start()

    def fwd_copies(j):
        return (
            remote(kv.at[j, chip_rows(left), lo], kv.at[j, chip_rows(left), lo],
                   fwd_send.at[j, 0], fwd_recv.at[j, 0], right_dev),
            remote(kv.at[j, chip_rows(right), hi], kv.at[j, chip_rows(right), hi],
                   fwd_send.at[j, 1], fwd_recv.at[j, 1], left_dev),
        )

    def forward(j):
        a, b = fwd_copies(j)
        landed(kv.at[j, chip_rows(left), lo], first_recv.at[j, 0])
        a.start()
        landed(kv.at[j, chip_rows(right), hi], first_recv.at[j, 1])
        b.start()

    def gathered(j):
        for c in own_copies(j):
            c.wait()
        landed(kv.at[j, block_rows(chip, 1 - core), :], sib_recv.at[j])
        landed(kv.at[j, chip_rows(right), lo], first_recv.at[j, 2])
        landed(kv.at[j, chip_rows(left), hi], first_recv.at[j, 3])
        landed(kv.at[j, chip_rows(far), lo], fwd_recv.at[j, 0])
        landed(kv.at[j, chip_rows(far), hi], fwd_recv.at[j, 1])

    def tail_copy(j):
        return remote(tail_send.at[j], kv.at[j, pl.ds(BLOCK, TAIL), :], tail_ssem.at[j], tail_rsem.at[j], after_dev)

    def send_tail(j):
        tail_send[j] = dot(take[...], kv[j, :BLOCK, :]).astype(BF16)
        tail_copy(j).start()

    def back_copy(j):
        return remote(back_send.at[j], back_recv.at[j], back_ssem.at[j], back_rsem.at[j], before_dev)

    def hop(j, n):
        dev = right_dev if n in (0, 3, 4) else left_dev
        return remote(hop_send.at[j, n], hop_recv.at[j, n], hop_ssem.at[j, n], hop_rsem.at[j, n], dev)

    def send_hop(j, n, value):
        hop_send[j, n] = value.astype(BF16)
        hop(j, n).start()

    def take_hop(j, n):
        hop(j, n).wait_recv()
        return hop_recv[j, n].astype(F32)

    def hops_first(j):
        s = j % 2
        back_copy(j).wait_recv()
        acc[s, :BLOCK, :] += dot(give[...], back_recv[j])
        send_hop(j, 0, acc[s, chip_rows(far), :HEAD])
        send_hop(j, 1, acc[s, chip_rows(far), HEAD:])
        send_hop(j, 2, acc[s, chip_rows(left), :HEAD])
        send_hop(j, 3, acc[s, chip_rows(right), HEAD:])

    def hops_second(j):
        s = j % 2
        send_hop(j, 4, acc[s, chip_rows(right), :HEAD] + take_hop(j, 0))
        send_hop(j, 5, acc[s, chip_rows(left), HEAD:] + take_hop(j, 1))

    def kv_copies(j):
        own, other = [], []
        for n, (dst, part) in enumerate(((dk_out, lo), (dv_out, hi))):
            cols = head_cols(core, j)
            own.append(pltpu.make_async_copy(out_stage.at[j, own_rows, part], dst.at[:, cols], kv_own.at[j, n]))
            other.append(
                remote(out_stage.at[j, sib_rows, part], dst.at[:, cols], kv_ssem.at[j, n], kv_rsem.at[j, n], sib_dev)
            )
        return own, other

    def hops_last(j):
        s = j % 2
        out_stage[j, :, :HEAD] = (acc[s, chip_rows(chip), :HEAD] + take_hop(j, 2) + take_hop(j, 4)).astype(BF16)
        out_stage[j, :, HEAD:] = (acc[s, chip_rows(chip), HEAD:] + take_hop(j, 3) + take_hop(j, 5)).astype(BF16)
        own, other = kv_copies(j)
        for c in own + other:
            c.start()

    def dq_copies(j):
        cols = tile((core * HEADS + j) * GROUP * HEAD, GROUP * HEAD)
        return (
            pltpu.make_async_copy(dq.at[j, own_rows, :], dq_out.at[:, cols], dq_own.at[j]),
            remote(dq.at[j, sib_rows, :], dq_out.at[:, cols], dq_ssem.at[j], dq_rsem.at[j], sib_dev),
        )

    start_first(0)
    swaps = [
        remote(src.at[:, sib_cols], dst.at[own_rows, :], pair_send.at[i], pair_recv.at[i], sib_dev)
        for i, (src, dst) in enumerate(pairs)
    ]
    for c in swaps:
        c.start()

    order_f = order[...].astype(F32)
    column = jnp.broadcast_to(order_f, (HEAD, BLOCK)).T
    mine = order[:, chip_rows(chip)].astype(F32)
    lane = lax.broadcasted_iota(jnp.int32, (BLOCK, HEAD), 1).astype(F32)
    for half in range(2):
        cols = slice(half * HEAD, (half + 1) * HEAD)
        bias[:BLOCK, cols] = jnp.where(column <= mine[:, cols], 0.0, MASKED)
        give[:, cols] = jnp.where(column == lane + float(BLOCK - TAIL + half * HEAD), 1.0, 0.0).astype(BF16)
    bias[BLOCK:, :] = jnp.full((TAIL, CHIP_ROWS), jnp.where(block > 0, 0.0, MASKED), F32)
    place = lax.broadcasted_iota(jnp.int32, (TAIL, BLOCK), 0).astype(F32)
    take[...] = jnp.where(order_f == place + float(BLOCK - TAIL), 1.0, 0.0).astype(BF16)

    forward(0)
    start_first(1)

    for c in loads:
        c.wait()
    for c in swaps:
        c.wait_recv()

    def delta_of(n, _):
        cols = tile(n * HEAD, HEAD)
        product = o[:, cols].astype(F32) * g[:, cols].astype(F32)
        delta[n] = jnp.sum(product.T, axis=0, keepdims=True)
        return 0

    lax.fori_loop(0, GROUP * HEADS, delta_of, 0)

    gathered(0)
    send_tail(0)
    forward(1)
    start_first(2)

    def step(n, _):
        j = n // GROUP
        a = n % GROUP

        @pl.when(a == 0)
        def _():
            tail_copy(j).wait_recv()

        cols = tile(n * HEAD, HEAD)
        lanes = tile(a * CHIP_ROWS, CHIP_ROWS)
        keys = kv[j, :, :HEAD]
        values = kv[j, :, HEAD:]
        s = dot(keys, q[:, cols], NT) + bias[...]
        top = jnp.max(s, axis=0, keepdims=True)
        e = jnp.exp2((s - top) * EXP_SCALE)
        p = e * (1.0 / jnp.sum(e, axis=0, keepdims=True))
        probs[:, lanes] = p.astype(BF16)
        dp = dot(values, g[:, cols], NT)
        ds = (p * (dp - delta[n])).astype(BF16)
        dscore[:, lanes] = ds
        dq[j, :, tile(a * HEAD, HEAD)] = (dot(ds, keys, TN) * SCALE).astype(BF16)

        @pl.when((a == 0) & (j >= 1))
        def _():
            hops_first(j - 1)

        @pl.when((a == 1) & (j == 0))
        def _():
            start_first(3)

        @pl.when((a == 2) & (j >= 1))
        def _():
            hops_second(j - 1)

        @pl.when((a == 2) & (j <= 2))
        def _():
            gathered(j + 1)
            send_tail(j + 1)

            @pl.when(j <= 1)
            def _():
                forward(j + 2)

        @pl.when(a == 3)
        def _():
            s = j % 2
            wide_q = tile(j * GROUP * HEAD, GROUP * HEAD)
            qs = q[:, wide_q]
            gs = g[:, wide_q]
            rows_q = jnp.concatenate([qs[:, i * HEAD : (i + 1) * HEAD] for i in range(GROUP)], axis=0)
            rows_g = jnp.concatenate([gs[:, i * HEAD : (i + 1) * HEAD] for i in range(GROUP)], axis=0)
            acc[s, :, :HEAD] = dot(dscore[...], rows_q) * SCALE
            acc[s, :, HEAD:] = dot(probs[...], rows_g)
            back_send[j] = acc[s, BLOCK:, :].astype(BF16)
            back_copy(j).start()
            for c in dq_copies(j):
                c.start()

            @pl.when(j >= 1)
            def _():
                hops_last(j - 1)

        return 0

    lax.fori_loop(0, GROUP * HEADS, step, 0)
    hops_first(HEADS - 1)
    hops_second(HEADS - 1)
    hops_last(HEADS - 1)

    for c in swaps:
        c.wait_send()

    def finish(j, _):
        for c in first_copies(j) + sib_copies(j):
            c.wait_send()
        for c in fwd_copies(j):
            c.wait_send()
        tail_copy(j).wait_send()
        back_copy(j).wait_send()
        for n in range(6):
            hop(j, n).wait_send()
        own, other = dq_copies(j)
        own.wait()
        other.wait()
        own, other = kv_copies(j)
        for c in own + other:
            c.wait()
        return 0

    lax.fori_loop(0, HEADS, finish, 0)


def body(queries, keys, values, output, gradient, order):
    any_spec = pl.BlockSpec(memory_space=pl.ANY)
    wide = GROUP * HEADS * HEAD
    dma = pltpu.SemaphoreType.DMA
    return pl.pallas_call(
        kernel,
        out_shape=(
            jax.ShapeDtypeStruct(queries.shape, BF16),
            jax.ShapeDtypeStruct(keys.shape, BF16),
            jax.ShapeDtypeStruct(values.shape, BF16),
        ),
        in_specs=[any_spec] * 5 + [pl.BlockSpec(memory_space=pltpu.VMEM)],
        out_specs=[any_spec] * 3,
        scratch_shapes=[
            pltpu.VMEM((CHIP_ROWS, wide), BF16),
            pltpu.VMEM((CHIP_ROWS, wide), BF16),
            pltpu.VMEM((CHIP_ROWS, wide), BF16),
            pltpu.VMEM((HEADS, KEYS, 2 * HEAD), BF16),
            pltpu.VMEM((KEYS, CHIP_ROWS), F32),
            pltpu.VMEM((TAIL, BLOCK), BF16),
            pltpu.VMEM((BLOCK, TAIL), BF16),
            pltpu.VMEM((GROUP * HEADS, 1, CHIP_ROWS), F32),
            pltpu.VMEM((KEYS, GROUP * CHIP_ROWS), BF16),
            pltpu.VMEM((KEYS, GROUP * CHIP_ROWS), BF16),
            pltpu.VMEM((2, KEYS, 2 * HEAD), F32),
            pltpu.VMEM((HEADS, CHIP_ROWS, GROUP * HEAD), BF16),
            pltpu.VMEM((HEADS, TAIL, 2 * HEAD), BF16),
            pltpu.VMEM((HEADS, TAIL, 2 * HEAD), BF16),
            pltpu.VMEM((HEADS, TAIL, 2 * HEAD), BF16),
            pltpu.VMEM((HEADS, 6, CHIP_ROWS, HEAD), BF16),
            pltpu.VMEM((HEADS, 6, CHIP_ROWS, HEAD), BF16),
            pltpu.VMEM((HEADS, CHIP_ROWS, 2 * HEAD), BF16),
            dma((3,)), dma((HEADS, 2)), dma((3,)), dma((3,)),
            dma((HEADS, 8)), dma((HEADS, 4)), dma((HEADS, 2)), dma((HEADS,)), dma((HEADS, 2)), dma((HEADS, 2)),
            dma((HEADS,)), dma((HEADS,)), dma((HEADS,)), dma((HEADS,)), dma((HEADS, 6)), dma((HEADS, 6)),
            dma((HEADS,)), dma((HEADS,)), dma((HEADS,)), dma((HEADS, 2)), dma((HEADS, 2)), dma((HEADS, 2)),
        ],
        compiler_params=pltpu.CompilerParams(
            collective_id=0, has_side_effects=True, vmem_limit_bytes=48 * 2**20
        ),
        name="banded_attention_grad",
    )(queries, keys, values, output, gradient, order)


def solution(mesh):
    spec = P(("ctx", "head"), None)
    return jax.shard_map(
        body,
        mesh=mesh,
        in_specs=(spec,) * 5 + (P("ctx", None),),
        out_specs=(spec,) * 3,
        check_vma=False,
    )
```

time: 306 us -> 127 us (0.42)
  the two profiles are of different devices: /device:TPU:8 before, /device:TPU:1 now
where the time goes in v1:
time: 127 us
  Pallas kernels  117 us (92%)
  local copies, waits for them, and re-layouts  8.63 us (7%)
    pallas_call x1, Pallas kernels, body(): pl.pallas_call(kernel, out_shape=(jax.ShapeDtypeStruct(queries.shape, BF1...  117 us
    unnamed x15, local copies, waits for them, and re-layouts  8.63 us

profile of v1, /device:TPU:1, one launch (start us, length us, event | category | flops | bytes accessed | tf_op | source)
XLA Modules:
  0.0 126.6 jit_solution(4221589323362543409)
XLA Ops:
  0.6 0.0 copy-start
  0.6 1.2 copy-done
  1.9 0.0 copy-start.1
  1.9 1.2 copy-done.1
  3.1 0.0 copy-start.2
  3.1 1.2 copy-done.2
  4.3 0.0 copy-start.3
  4.3 0.9 copy-done.3
  5.3 0.0 copy-start.4
  5.3 0.9 copy-done.4
  6.2 0.0 copy-start.5
  6.2 0.7 copy-done.5
  6.9 117.3 %banded_attention_grad.1 = (bf16[128,4096]{1,0:T(8,128)(2,1)S(1)}, bf16[128,1024]{1,0:T(8,128)(2,1)S(1)}, bf16[128,1024]{1,0:T(8,128)(2,1)S(1)}) custom-call(bf16[128,4096]{1,0:T(8,128)(2,1)S(1)} %copy-done, bf16[128,1024]{1,0:T(8,128)(2,1)S(1)} %copy-done.3, bf16[128,1024]{1,0:T(8,128)(2,1)S(1)} %copy-done.4, bf16[128,4096]{1,0:T(8,128)(2,1)S(1)} %copy-done.1, ...), custom_call_target="tpu_custom_call" | custom-call | tf_op jit(solution)/shard_map/banded_attention_grad/pallas_call | solution.py:353
  124.2 1.0 copy.12
  125.2 0.7 copy.13
  125.9 0.7 copy.14
Async XLA Ops:
  0.6 1.2 copy-start
  1.9 1.2 copy-start.1
  3.1 1.2 copy-start.2
  4.3 0.9 copy-start.3
  5.3 0.9 copy-start.4
  6.2 0.7 copy-start.5

commit v2 on v1

--- a/solution.py
+++ b/solution.py
@@ -15,6 +15,7 @@
 BLOCK = 1024
 TAIL = 256
 KEYS = BLOCK + TAIL
+PART = 256
 SCALE = 1.0 / math.sqrt(HEAD)
 EXP_SCALE = SCALE * math.log2(math.e)
 MASKED = -1e30
@@ -37,7 +38,7 @@
 def kernel(
     q_in, k_in, v_in, o_in, g_in, order,
     dq_out, dk_out, dv_out,
-    q, g, o, kv, bias, take, give, delta, probs, dscore, acc, dq,
+    q, g, o, kv, bias, take, give, delta, scores, keys_t, probs, dscore, acc, dq,
     tail_send, back_send, back_recv, hop_send, hop_recv, out_stage,
     load_sem, own_sem, pair_send, pair_recv,
     first_send, first_recv, sib_send, sib_recv, fwd_send, fwd_recv,
@@ -51,9 +52,17 @@
     right, left, far = (chip + 1) % 4, (chip + 3) % 4, (chip + 2) % 4
     sib = chip * 2 + 1 - core
     after, before = (block + 1) % 64, (block + 63) % 64
+    bend_after = (block % 8 + 1) // 8 * (block // 8 % 2 * 2 - 1)
+    bend_before = (before % 8 + 1) // 8 * (before // 8 % 2 * 2 - 1)
     lo, hi = pl.ds(0, HEAD), pl.ds(HEAD, HEAD)
     right_dev, left_dev, sib_dev = {"head": right * 2 + core}, {"head": left * 2 + core}, {"head": sib}
-    after_dev, before_dev = {"ctx": after}, {"ctx": before}
+
+    def after_dev(n):
+        return {"head": (chip + 4 + n * bend_after) % 4 * 2 + core, "ctx": after}
+
+    def before_dev(n):
+        return {"head": (chip + 4 - n * bend_before) % 4 * 2 + core, "ctx": before}
+
     own_rows = tile(core * ROWS, ROWS)
     sib_rows = tile((1 - core) * ROWS, ROWS)
     wide = GROUP * HEADS * HEAD
@@ -88,7 +97,7 @@
     barrier = pltpu.get_barrier_semaphore()
     for dev in (
         {"head": right * 2}, {"head": right * 2 + 1}, {"head": left * 2}, {"head": left * 2 + 1},
-        sib_dev, after_dev, before_dev,
+        sib_dev, before_dev(0), before_dev(1),
     ):
         pl.semaphore_signal(barrier, inc=1, device_id=dev, device_id_type=MESH)
     pl.semaphore_wait(barrier, 7)
@@ -152,15 +161,26 @@
         landed(kv.at[j, chip_rows(far), lo], fwd_recv.at[j, 0])
         landed(kv.at[j, chip_rows(far), hi], fwd_recv.at[j, 1])
 
-    def tail_copy(j):
-        return remote(tail_send.at[j], kv.at[j, pl.ds(BLOCK, TAIL), :], tail_ssem.at[j], tail_rsem.at[j], after_dev)
+    halves = (slice(0, HEAD), slice(HEAD, 2 * HEAD))
+
+    def tail_copies(j):
+        return [
+            remote(tail_send.at[j, n], kv.at[j, pl.ds(BLOCK, TAIL), part],
+                   tail_ssem.at[j, n], tail_rsem.at[j, n], after_dev(n))
+            for n, part in enumerate((lo, hi))
+        ]
 
     def send_tail(j):
-        tail_send[j] = dot(take[...], kv[j, :BLOCK, :]).astype(BF16)
-        tail_copy(j).start()
-
-    def back_copy(j):
-        return remote(back_send.at[j], back_recv.at[j], back_ssem.at[j], back_rsem.at[j], before_dev)
+        rows = dot(take[...], kv[j, :BLOCK, :]).astype(BF16)
+        for n, c in enumerate(tail_copies(j)):
+            tail_send[j, n] = rows[:, halves[n]]
+            c.start()
+
+    def back_copies(j):
+        return [
+            remote(back_send.at[j, n], back_recv.at[j, n], back_ssem.at[j, n], back_rsem.at[j, n], before_dev(n))
+            for n in range(2)
+        ]
 
     def hop(j, n):
         dev = right_dev if n in (0, 3, 4) else left_dev
@@ -175,16 +195,18 @@
         return hop_recv[j, n].astype(F32)
 
     def hops_first(j):
-        s = j % 2
-        back_copy(j).wait_recv()
-        acc[s, :BLOCK, :] += dot(give[...], back_recv[j])
+        s = j
+        for c in back_copies(j):
+            c.wait_recv()
+        back = jnp.concatenate([back_recv[j, 0], back_recv[j, 1]], axis=1)
+        acc[s] += dot(give[...], back)
         send_hop(j, 0, acc[s, chip_rows(far), :HEAD])
         send_hop(j, 1, acc[s, chip_rows(far), HEAD:])
         send_hop(j, 2, acc[s, chip_rows(left), :HEAD])
         send_hop(j, 3, acc[s, chip_rows(right), HEAD:])
 
     def hops_second(j):
-        s = j % 2
+        s = j
         send_hop(j, 4, acc[s, chip_rows(right), :HEAD] + take_hop(j, 0))
         send_hop(j, 5, acc[s, chip_rows(left), HEAD:] + take_hop(j, 1))
 
@@ -199,7 +221,7 @@
         return own, other
 
     def hops_last(j):
-        s = j % 2
+        s = j
         out_stage[j, :, :HEAD] = (acc[s, chip_rows(chip), :HEAD] + take_hop(j, 2) + take_hop(j, 4)).astype(BF16)
         out_stage[j, :, HEAD:] = (acc[s, chip_rows(chip), HEAD:] + take_hop(j, 3) + take_hop(j, 5)).astype(BF16)
         own, other = kv_copies(j)
@@ -222,6 +244,8 @@
         c.start()
 
     order_f = order[...].astype(F32)
+    place = lax.broadcasted_iota(jnp.int32, (TAIL, BLOCK), 0).astype(F32)
+    take[...] = jnp.where(order_f == place + float(BLOCK - TAIL), 1.0, 0.0).astype(BF16)
     column = jnp.broadcast_to(order_f, (HEAD, BLOCK)).T
     mine = order[:, chip_rows(chip)].astype(F32)
     lane = lax.broadcasted_iota(jnp.int32, (BLOCK, HEAD), 1).astype(F32)
@@ -230,8 +254,6 @@
         bias[:BLOCK, cols] = jnp.where(column <= mine[:, cols], 0.0, MASKED)
         give[:, cols] = jnp.where(column == lane + float(BLOCK - TAIL + half * HEAD), 1.0, 0.0).astype(BF16)
     bias[BLOCK:, :] = jnp.full((TAIL, CHIP_ROWS), jnp.where(block > 0, 0.0, MASKED), F32)
-    place = lax.broadcasted_iota(jnp.int32, (TAIL, BLOCK), 0).astype(F32)
-    take[...] = jnp.where(order_f == place + float(BLOCK - TAIL), 1.0, 0.0).astype(BF16)
 
     forward(0)
     start_first(1)
@@ -251,77 +273,89 @@
 
     gathered(0)
     send_tail(0)
+    start_first(2)
     forward(1)
-    start_first(2)
-
-    def step(n, _):
-        j = n // GROUP
-        a = n % GROUP
-
-        @pl.when(a == 0)
+    start_first(3)
+    gathered(1)
+    send_tail(1)
+    forward(2)
+
+    def step(j, _):
+        for c in tail_copies(j):
+            c.wait_recv()
+        keys_t[...] = kv[j, :, :HEAD].T
+        for a in range(GROUP):
+            n = j * GROUP + a
+            cols = tile(n * HEAD, HEAD)
+            lanes = slice(a * CHIP_ROWS, (a + 1) * CHIP_ROWS)
+            u = a % 2
+            query = q[:, cols]
+            top = None
+            for t in range(KEYS // PART):
+                r = slice(t * PART, (t + 1) * PART)
+                part = dot(kv[j, r, :HEAD], query, NT) + bias[r, :]
+                scores[u, r, :] = part
+                part = jnp.max(part.reshape(PART // 8, 8, CHIP_ROWS), axis=0)
+                top = part if top is None else jnp.maximum(top, part)
+            top = jnp.max(top, axis=0, keepdims=True)
+            total = None
+            for t in range(KEYS // PART):
+                r = slice(t * PART, (t + 1) * PART)
+                part = jnp.exp2((scores[u, r, :] - top) * EXP_SCALE)
+                scores[u, r, :] = part
+                part = jnp.sum(part.reshape(PART // 8, 8, CHIP_ROWS), axis=0)
+                total = part if total is None else total + part
+            share = 1.0 / jnp.sum(total, axis=0, keepdims=True)
+            grad = g[:, cols]
+            shift = delta[n]
+            for t in range(KEYS // PART):
+                r = slice(t * PART, (t + 1) * PART)
+                p = scores[u, r, :] * share
+                probs[r, lanes] = p.astype(BF16)
+                dp = dot(kv[j, r, HEAD:], grad, NT)
+                dscore[r, lanes] = (p * (dp - shift)).astype(BF16)
+        wide_q = tile(j * GROUP * HEAD, GROUP * HEAD)
+        qs = q[:, wide_q]
+        gs = g[:, wide_q]
+        rows_q = jnp.concatenate([qs[:, i * HEAD : (i + 1) * HEAD] for i in range(GROUP)], axis=0)
+        rows_g = jnp.concatenate([gs[:, i * HEAD : (i + 1) * HEAD] for i in range(GROUP)], axis=0)
+        back_send[j, 0] = (dot(dscore[BLOCK:, :], rows_q) * SCALE).astype(BF16)
+        back_send[j, 1] = dot(probs[BLOCK:, :], rows_g).astype(BF16)
+        for c in back_copies(j):
+            c.start()
+        acc[j, :, :HEAD] = dot(dscore[:BLOCK, :], rows_q) * SCALE
+        acc[j, :, HEAD:] = dot(probs[:BLOCK, :], rows_g)
+        dq_t = dot(keys_t[...], dscore[...])
+        for a in range(GROUP):
+            dq[j, :, a * HEAD : (a + 1) * HEAD] = (dq_t[:, a * CHIP_ROWS : (a + 1) * CHIP_ROWS].T * SCALE).astype(BF16)
+        for c in dq_copies(j):
+            c.start()
+
+        @pl.when(j == 0)
         def _():
-            tail_copy(j).wait_recv()
-
-        cols = tile(n * HEAD, HEAD)
-        lanes = tile(a * CHIP_ROWS, CHIP_ROWS)
-        keys = kv[j, :, :HEAD]
-        values = kv[j, :, HEAD:]
-        s = dot(keys, q[:, cols], NT) + bias[...]
-        top = jnp.max(s, axis=0, keepdims=True)
-        e = jnp.exp2((s - top) * EXP_SCALE)
-        p = e * (1.0 / jnp.sum(e, axis=0, keepdims=True))
-        probs[:, lanes] = p.astype(BF16)
-        dp = dot(values, g[:, cols], NT)
-        ds = (p * (dp - delta[n])).astype(BF16)
-        dscore[:, lanes] = ds
-        dq[j, :, tile(a * HEAD, HEAD)] = (dot(ds, keys, TN) * SCALE).astype(BF16)
-
-        @pl.when((a == 0) & (j >= 1))
+            forward(3)
+
+        @pl.when((j == 0) | (j == 2))
+        def _():
+            gathered(j // 2 + 2)
+            send_tail(j // 2 + 2)
+
+        @pl.when(j >= 1)
         def _():
             hops_first(j - 1)
 
-        @pl.when((a == 1) & (j == 0))
-        def _():
-            start_first(3)
-
-        @pl.when((a == 2) & (j >= 1))
-        def _():
-            hops_second(j - 1)
-
-        @pl.when((a == 2) & (j <= 2))
-        def _():
-            gathered(j + 1)
-            send_tail(j + 1)
-
-            @pl.when(j <= 1)
-            def _():
-                forward(j + 2)
-
-        @pl.when(a == 3)
-        def _():
-            s = j % 2
-            wide_q = tile(j * GROUP * HEAD, GROUP * HEAD)
-            qs = q[:, wide_q]
-            gs = g[:, wide_q]
-            rows_q = jnp.concatenate([qs[:, i * HEAD : (i + 1) * HEAD] for i in range(GROUP)], axis=0)
-            rows_g = jnp.concatenate([gs[:, i * HEAD : (i + 1) * HEAD] for i in range(GROUP)], axis=0)
-            acc[s, :, :HEAD] = dot(dscore[...], rows_q) * SCALE
-            acc[s, :, HEAD:] = dot(probs[...], rows_g)
-            back_send[j] = acc[s, BLOCK:, :].astype(BF16)
-            back_copy(j).start()
-            for c in dq_copies(j):
-                c.start()
-
-            @pl.when(j >= 1)
-            def _():
-                hops_last(j - 1)
-
         return 0
 
-    lax.fori_loop(0, GROUP * HEADS, step, 0)
-    hops_first(HEADS - 1)
-    hops_second(HEADS - 1)
-    hops_last(HEADS - 1)
+    lax.fori_loop(0, HEADS, step, 0)
+    hops_second(0)
+    hops_second(1)
+    hops_first(3)
+    hops_last(0)
+    hops_second(2)
+    hops_last(1)
+    hops_second(3)
+    hops_last(2)
+    hops_last(3)
 
     for c in swaps:
         c.wait_send()
@@ -331,8 +365,8 @@
             c.wait_send()
         for c in fwd_copies(j):
             c.wait_send()
-        tail_copy(j).wait_send()
-        back_copy(j).wait_send()
+        for c in tail_copies(j) + back_copies(j):
+            c.wait_send()
         for n in range(6):
             hop(j, n).wait_send()
         own, other = dq_copies(j)
@@ -368,23 +402,25 @@
             pltpu.VMEM((TAIL, BLOCK), BF16),
             pltpu.VMEM((BLOCK, TAIL), BF16),
             pltpu.VMEM((GROUP * HEADS, 1, CHIP_ROWS), F32),
+            pltpu.VMEM((2, KEYS, CHIP_ROWS), F32),
+            pltpu.VMEM((HEAD, KEYS), BF16),
             pltpu.VMEM((KEYS, GROUP * CHIP_ROWS), BF16),
             pltpu.VMEM((KEYS, GROUP * CHIP_ROWS), BF16),
-            pltpu.VMEM((2, KEYS, 2 * HEAD), F32),
+            pltpu.VMEM((HEADS, BLOCK, 2 * HEAD), F32),
             pltpu.VMEM((HEADS, CHIP_ROWS, GROUP * HEAD), BF16),
-            pltpu.VMEM((HEADS, TAIL, 2 * HEAD), BF16),
-            pltpu.VMEM((HEADS, TAIL, 2 * HEAD), BF16),
-            pltpu.VMEM((HEADS, TAIL, 2 * HEAD), BF16),
+            pltpu.VMEM((HEADS, 2, TAIL, HEAD), BF16),
+            pltpu.VMEM((HEADS, 2, TAIL, HEAD), BF16),
+            pltpu.VMEM((HEADS, 2, TAIL, HEAD), BF16),
             pltpu.VMEM((HEADS, 6, CHIP_ROWS, HEAD), BF16),
             pltpu.VMEM((HEADS, 6, CHIP_ROWS, HEAD), BF16),
             pltpu.VMEM((HEADS, CHIP_ROWS, 2 * HEAD), BF16),
             dma((3,)), dma((HEADS, 2)), dma((3,)), dma((3,)),
             dma((HEADS, 8)), dma((HEADS, 4)), dma((HEADS, 2)), dma((HEADS,)), dma((HEADS, 2)), dma((HEADS, 2)),
-            dma((HEADS,)), dma((HEADS,)), dma((HEADS,)), dma((HEADS,)), dma((HEADS, 6)), dma((HEADS, 6)),
+            dma((HEADS, 2)), dma((HEADS, 2)), dma((HEADS, 2)), dma((HEADS, 2)), dma((HEADS, 6)), dma((HEADS, 6)),
             dma((HEADS,)), dma((HEADS,)), dma((HEADS,)), dma((HEADS, 2)), dma((HEADS, 2)), dma((HEADS, 2)),
         ],
         compiler_params=pltpu.CompilerParams(
-            collective_id=0, has_side_effects=True, vmem_limit_bytes=48 * 2**20
+            collective_id=0, has_side_effects=True, vmem_limit_bytes=62 * 2**20
         ),
         name="banded_attention_grad",
     )(queries, keys, values, output, gradient, order)

time: 127 us -> 109 us (0.86)
  Pallas kernels: 117 us -> 104 us
  local copies, waits for them, and re-layouts: 8.63 us -> 4.08 us
    pallas_call x1, Pallas kernels: 117 us -> 104 us  [body(): pl.pallas_call(kernel, out_shape=(jax.ShapeDtypeStruct(queries.shape, BF1...]
    unnamed x15 -> x7, local copies, waits for them, and re-layouts: 8.63 us -> 4.08 us
where the time goes in v2:
time: 109 us
  Pallas kernels  104 us (95%)
  local copies, waits for them, and re-layouts  4.08 us (4%)
    pallas_call x1, Pallas kernels, body(): pl.pallas_call(kernel, out_shape=(jax.ShapeDtypeStruct(queries.shape, BF1...  104 us
    unnamed x7, local copies, waits for them, and re-layouts  4.08 us

profile of v2, /device:TPU:1, one launch (start us, length us, event | category | flops | bytes accessed | tf_op | source)
XLA Modules:
  0.0 108.9 jit_solution(6927784882453120427)
XLA Ops:
  0.6 104.1 %banded_attention_grad.1 = (bf16[128,4096]{1,0:T(8,128)(2,1)}, bf16[128,1024]{1,0:T(8,128)(2,1)}, bf16[128,1024]{1,0:T(8,128)(2,1)}) custom-call(bf16[128,4096]{1,0:T(8,128)(2,1)} %q_in.1, bf16[128,1024]{1,0:T(8,128)(2,1)} %k_in.1, bf16[128,1024]{1,0:T(8,128)(2,1)} %v_in.1, bf16[128,4096]{1,0:T(8,128)(2,1)} %o_in.1, bf16[128,4096]{1,0:T(8,128)(2,1)} %g_in.1, ...), custom_call_target="tpu_custom_call" | custom-call | tf_op jit(solution)/shard_map/banded_attention_grad/pallas_call | solution.py:387
  104.8 0.0 copy-start.1
  104.8 2.3 %copy.12 = bf16[128,4096]{1,0:T(8,128)(2,1)} copy(bf16[128,4096]{1,0:T(8,128)(2,1)} %get-tuple-element.6) | data formatting | bytes 2097152
  107.1 0.0 copy-done.1
  107.1 0.0 copy-start
  107.1 0.7 copy.13
  107.8 0.3 copy-done
  108.2 0.7 copy.14
Async XLA Ops:
  104.8 2.3 %copy-start.1 = (bf16[128,1024]{1,0:T(8,128)(2,1)S(1)}, bf16[128,1024]{1,0:T(8,128)(2,1)}, u32[]{:S(2)}) copy-start(bf16[128,1024]{1,0:T(8,128)(2,1)} %get-tuple-element.7) | copy-start | bytes 786436
  107.1 1.0 copy-start

commit v3 on v2

--- a/solution.py
+++ b/solution.py
@@ -54,6 +54,7 @@
     after, before = (block + 1) % 64, (block + 63) % 64
     bend_after = (block % 8 + 1) // 8 * (block // 8 % 2 * 2 - 1)
     bend_before = (before % 8 + 1) // 8 * (before // 8 % 2 * 2 - 1)
+    eager = 1 - (block % 8 + 7) // 8
     lo, hi = pl.ds(0, HEAD), pl.ds(HEAD, HEAD)
     right_dev, left_dev, sib_dev = {"head": right * 2 + core}, {"head": left * 2 + core}, {"head": sib}
 
@@ -102,11 +103,11 @@
         pl.semaphore_signal(barrier, inc=1, device_id=dev, device_id_type=MESH)
     pl.semaphore_wait(barrier, 7)
 
-    def first_copies(j):
+    def first_copies(j, which=(0, 1, 2, 3)):
+        kinds = ((k_in, lo, right), (v_in, hi, left), (k_in, lo, left), (v_in, hi, right))
         out = []
-        for n, (src, part, to) in enumerate(
-            ((k_in, lo, right), (v_in, hi, left), (k_in, lo, left), (v_in, hi, right))
-        ):
+        for n in which:
+            src, part, to = kinds[n]
             for k in range(2):
                 out.append(
                     remote(
@@ -133,8 +134,12 @@
             for n, (src, part) in enumerate(((k_in, lo), (v_in, hi)))
         ]
 
-    def start_first(j):
-        for c in first_copies(j) + sib_copies(j) + own_copies(j):
+    def start_onward(j):
+        for c in first_copies(j, (0, 1)) + sib_copies(j) + own_copies(j):
+            c.start()
+
+    def start_near(j):
+        for c in first_copies(j, (2, 3)):
             c.start()
 
     def fwd_copies(j):
@@ -195,15 +200,23 @@
         return hop_recv[j, n].astype(F32)
 
     def hops_first(j):
-        s = j
         for c in back_copies(j):
             c.wait_recv()
         back = jnp.concatenate([back_recv[j, 0], back_recv[j, 1]], axis=1)
-        acc[s] += dot(give[...], back)
-        send_hop(j, 0, acc[s, chip_rows(far), :HEAD])
-        send_hop(j, 1, acc[s, chip_rows(far), HEAD:])
-        send_hop(j, 2, acc[s, chip_rows(left), :HEAD])
-        send_hop(j, 3, acc[s, chip_rows(right), HEAD:])
+
+        def whole(c):
+            return acc[j, chip_rows(c), :] + dot(give[chip_rows(c), :], back)
+
+        part = whole(far)
+        send_hop(j, 0, part[:, :HEAD])
+        send_hop(j, 1, part[:, HEAD:])
+        part = whole(left)
+        send_hop(j, 2, part[:, :HEAD])
+        acc[j, chip_rows(left), HEAD:] = part[:, HEAD:]
+        part = whole(right)
+        send_hop(j, 3, part[:, HEAD:])
+        acc[j, chip_rows(right), :HEAD] = part[:, :HEAD]
+        acc[j, chip_rows(chip), :] = whole(chip)
 
     def hops_second(j):
         s = j
@@ -235,17 +248,24 @@
             remote(dq.at[j, sib_rows, :], dq_out.at[:, cols], dq_ssem.at[j], dq_rsem.at[j], sib_dev),
         )
 
-    start_first(0)
+    start_onward(0)
+    start_near(0)
     swaps = [
         remote(src.at[:, sib_cols], dst.at[own_rows, :], pair_send.at[i], pair_recv.at[i], sib_dev)
         for i, (src, dst) in enumerate(pairs)
     ]
     for c in swaps:
         c.start()
+    start_onward(1)
 
     order_f = order[...].astype(F32)
     place = lax.broadcasted_iota(jnp.int32, (TAIL, BLOCK), 0).astype(F32)
     take[...] = jnp.where(order_f == place + float(BLOCK - TAIL), 1.0, 0.0).astype(BF16)
+
+    forward(0)
+    start_near(1)
+    start_onward(2)
+
     column = jnp.broadcast_to(order_f, (HEAD, BLOCK)).T
     mine = order[:, chip_rows(chip)].astype(F32)
     lane = lax.broadcasted_iota(jnp.int32, (BLOCK, HEAD), 1).astype(F32)
@@ -255,8 +275,11 @@
         give[:, cols] = jnp.where(column == lane + float(BLOCK - TAIL + half * HEAD), 1.0, 0.0).astype(BF16)
     bias[BLOCK:, :] = jnp.full((TAIL, CHIP_ROWS), jnp.where(block > 0, 0.0, MASKED), F32)
 
-    forward(0)
-    start_first(1)
+    gathered(0)
+    send_tail(0)
+    forward(1)
+    start_near(2)
+    start_onward(3)
 
     for c in loads:
         c.wait()
@@ -271,14 +294,10 @@
 
     lax.fori_loop(0, GROUP * HEADS, delta_of, 0)
 
-    gathered(0)
-    send_tail(0)
-    start_first(2)
-    forward(1)
-    start_first(3)
+    forward(2)
+    start_near(3)
     gathered(1)
     send_tail(1)
-    forward(2)
 
     def step(j, _):
         for c in tail_copies(j):
@@ -335,26 +354,32 @@
         def _():
             forward(3)
 
-        @pl.when((j == 0) | (j == 2))
+        @pl.when(j + eager >= 1)
         def _():
-            gathered(j // 2 + 2)
-            send_tail(j // 2 + 2)
-
-        @pl.when(j >= 1)
+            hops_first(j - 1 + eager)
+
+        @pl.when(j <= 1)
         def _():
-            hops_first(j - 1)
+            gathered(j + 2)
+            send_tail(j + 2)
+
+        @pl.when(j + eager >= 2)
+        def _():
+            hops_second(j - 2 + eager)
 
         return 0
 
     lax.fori_loop(0, HEADS, step, 0)
-    hops_second(0)
-    hops_second(1)
-    hops_first(3)
     hops_last(0)
-    hops_second(2)
+
+    @pl.when(eager == 0)
+    def _():
+        hops_first(3)
+        hops_second(2)
+
     hops_last(1)
+    hops_last(2)
     hops_second(3)
-    hops_last(2)
     hops_last(3)
 
     for c in swaps:
@@ -380,11 +405,19 @@
     lax.fori_loop(0, HEADS, finish, 0)
 
 
+def settle(a, b, c, x, y, z, sem):
+    copies = [pltpu.make_async_copy(s, d, sem.at[i]) for i, (s, d) in enumerate(((a, x), (b, y), (c, z)))]
+    for copy in copies:
+        copy.start()
+    for copy in copies:
+        copy.wait()
+
+
 def body(queries, keys, values, output, gradient, order):
     any_spec = pl.BlockSpec(memory_space=pl.ANY)
     wide = GROUP * HEADS * HEAD
     dma = pltpu.SemaphoreType.DMA
-    return pl.pallas_call(
+    grads = pl.pallas_call(
         kernel,
         out_shape=(
             jax.ShapeDtypeStruct(queries.shape, BF16),
@@ -424,6 +457,14 @@
         ),
         name="banded_attention_grad",
     )(queries, keys, values, output, gradient, order)
+    return pl.pallas_call(
+        settle,
+        out_shape=tuple(jax.ShapeDtypeStruct(x.shape, BF16) for x in grads),
+        in_specs=[pl.BlockSpec(memory_space=pltpu.VMEM)] * 3,
+        out_specs=[any_spec] * 3,
+        scratch_shapes=[dma((3,))],
+        name="settle",
+    )(*grads)
 
 
 def solution(mesh):

time: 109 us -> 103 us (0.945)
  local copies, waits for them, and re-layouts: 4.08 us -> 0 us
  Pallas kernels: 104 us -> 102 us
    pallas_call x1, Pallas kernels: 104 us -> 99.9 us  [body(): pl.pallas_call(kernel, out_shape=(jax.ShapeDtypeStruct(queries.shape, BF1...]
    unnamed x7 -> x0, local copies, waits for them, and re-layouts: 4.08 us -> none
    pallas_call x0 -> x1, Pallas kernels: none -> 2.5 us  [body(): pl.pallas_call(settle, out_shape=tuple((jax.ShapeDtypeStruct(x.shape, BF1...]
where the time goes in v3:
time: 103 us
  Pallas kernels  102 us (99%)
    pallas_call x1, Pallas kernels, body(): pl.pallas_call(kernel, out_shape=(jax.ShapeDtypeStruct(queries.shape, BF1...  99.9 us
    pallas_call x1, Pallas kernels, body(): pl.pallas_call(settle, out_shape=tuple((jax.ShapeDtypeStruct(x.shape, BF1...  2.5 us

profile of v3, /device:TPU:1, one launch (start us, length us, event | category | flops | bytes accessed | tf_op | source)
XLA Modules:
  0.0 103.1 jit_solution(1720540497067255796)
XLA Ops:
  0.6 99.9 %banded_attention_grad.1 = (bf16[128,4096]{1,0:T(8,128)(2,1)}, bf16[128,1024]{1,0:T(8,128)(2,1)}, bf16[128,1024]{1,0:T(8,128)(2,1)}) custom-call(bf16[128,4096]{1,0:T(8,128)(2,1)} %q_in.1, bf16[128,1024]{1,0:T(8,128)(2,1)} %k_in.1, bf16[128,1024]{1,0:T(8,128)(2,1)} %v_in.1, bf16[128,4096]{1,0:T(8,128)(2,1)} %o_in.1, bf16[128,4096]{1,0:T(8,128)(2,1)} %g_in.1, ...), custom_call_target="tpu_custom_call" | custom-call | tf_op jit(solution)/shard_map/banded_attention_grad/pallas_call | solution.py:420
  100.6 2.5 %settle.1 = (bf16[128,4096]{1,0:T(8,128)(2,1)}, bf16[128,1024]{1,0:T(8,128)(2,1)}, bf16[128,1024]{1,0:T(8,128)(2,1)}) custom-call(bf16[128,4096]{1,0:T(8,128)(2,1)} %get-tuple-element.6.a, bf16[128,1024]{1,0:T(8,128)(2,1)} %get-tuple-element.7.b, bf16[128,1024]{1,0:T(8,128)(2,1)} %get-tuple-element.8.c), custom_call_target="tpu_custom_call" | custom-call | tf_op jit(solution)/shard_map/settle/pallas_call | solution.py:460

commit v4 on v3

--- a/solution.py
+++ b/solution.py
@@ -370,16 +370,16 @@
         return 0
 
     lax.fori_loop(0, HEADS, step, 0)
-    hops_last(0)
 
     @pl.when(eager == 0)
     def _():
         hops_first(3)
         hops_second(2)
 
+    hops_last(0)
+    hops_second(3)
     hops_last(1)
     hops_last(2)
-    hops_second(3)
     hops_last(3)
 
     for c in swaps:
@@ -405,12 +405,26 @@
     lax.fori_loop(0, HEADS, finish, 0)
 
 
-def settle(a, b, c, x, y, z, sem):
-    copies = [pltpu.make_async_copy(s, d, sem.at[i]) for i, (s, d) in enumerate(((a, x), (b, y), (c, z)))]
-    for copy in copies:
-        copy.start()
-    for copy in copies:
-        copy.wait()
+def settle(a, b, c, x, y, z, wide, keys, values, in_sem, out_sem):
+    pieces = []
+    for src, held, dst in ((a, wide, x), (b, keys, y), (c, values, z)):
+        step = min(src.shape[1], BLOCK)
+        for at in range(0, src.shape[1], step):
+            part = pl.ds(at, step)
+            n = len(pieces)
+            pieces.append(
+                (
+                    pltpu.make_async_copy(src.at[:, part], held.at[:, part], in_sem.at[n]),
+                    pltpu.make_async_copy(held.at[:, part], dst.at[:, part], out_sem.at[n]),
+                )
+            )
+    for come, _ in pieces:
+        come.start()
+    for come, go in pieces:
+        come.wait()
+        go.start()
+    for _, go in pieces:
+        go.wait()
 
 
 def body(queries, keys, values, output, gradient, order):
@@ -460,9 +474,10 @@
     return pl.pallas_call(
         settle,
         out_shape=tuple(jax.ShapeDtypeStruct(x.shape, BF16) for x in grads),
-        in_specs=[pl.BlockSpec(memory_space=pltpu.VMEM)] * 3,
+        in_specs=[any_spec] * 3,
         out_specs=[any_spec] * 3,
-        scratch_shapes=[dma((3,))],
+        scratch_shapes=[pltpu.VMEM(x.shape, BF16) for x in grads] + [dma((6,)), dma((6,))],
+        compiler_params=pltpu.CompilerParams(vmem_limit_bytes=62 * 2**20),
         name="settle",
     )(*grads)
 

time: 103 us -> 100 us (0.971)
  Pallas kernels: 102 us -> 99.3 us
    pallas_call x1, Pallas kernels: 99.9 us -> 97.1 us  [body(): pl.pallas_call(kernel, out_shape=(jax.ShapeDtypeStruct(queries.shape, BF1...]
where the time goes in v4:
time: 100 us
  Pallas kernels  99.3 us (99%)
    pallas_call x1, Pallas kernels, body(): pl.pallas_call(kernel, out_shape=(jax.ShapeDtypeStruct(queries.shape, BF1...  97.1 us
    pallas_call x1, Pallas kernels, body(): pl.pallas_call(settle, out_shape=tuple((jax.ShapeDtypeStruct(x.shape, BF1...  2.19 us

profile of v4, /device:TPU:1, one launch (start us, length us, event | category | flops | bytes accessed | tf_op | source)
XLA Modules:
  0.0 100.0 jit_solution(5634723836738592123)
XLA Ops:
  0.6 97.1 %banded_attention_grad.1 = (bf16[128,4096]{1,0:T(8,128)(2,1)}, bf16[128,1024]{1,0:T(8,128)(2,1)}, bf16[128,1024]{1,0:T(8,128)(2,1)}) custom-call(bf16[128,4096]{1,0:T(8,128)(2,1)} %q_in.1, bf16[128,1024]{1,0:T(8,128)(2,1)} %k_in.1, bf16[128,1024]{1,0:T(8,128)(2,1)} %v_in.1, bf16[128,4096]{1,0:T(8,128)(2,1)} %o_in.1, bf16[128,4096]{1,0:T(8,128)(2,1)} %g_in.1, ...), custom_call_target="tpu_custom_call" | custom-call | tf_op jit(solution)/shard_map/banded_attention_grad/pallas_call | solution.py:434
  97.8 2.2 %settle.1 = (bf16[128,4096]{1,0:T(8,128)(2,1)}, bf16[128,1024]{1,0:T(8,128)(2,1)}, bf16[128,1024]{1,0:T(8,128)(2,1)}) custom-call(bf16[128,4096]{1,0:T(8,128)(2,1)} %get-tuple-element.6.a, bf16[128,1024]{1,0:T(8,128)(2,1)} %get-tuple-element.7.b, bf16[128,1024]{1,0:T(8,128)(2,1)} %get-tuple-element.8.c), custom_call_target="tpu_custom_call" | custom-call | tf_op jit(solution)/shard_map/settle/pallas_call | solution.py:474

commit v5 on v4

--- a/solution.py
+++ b/solution.py
@@ -235,11 +235,12 @@
 
     def hops_last(j):
         s = j
-        out_stage[j, :, :HEAD] = (acc[s, chip_rows(chip), :HEAD] + take_hop(j, 2) + take_hop(j, 4)).astype(BF16)
-        out_stage[j, :, HEAD:] = (acc[s, chip_rows(chip), HEAD:] + take_hop(j, 3) + take_hop(j, 5)).astype(BF16)
         own, other = kv_copies(j)
-        for c in own + other:
-            c.start()
+        for n, (near, sums) in enumerate(((2, 4), (3, 5))):
+            value = acc[s, chip_rows(chip), halves[n]] + take_hop(j, near) + take_hop(j, sums)
+            out_stage[j, :, halves[n]] = value.astype(BF16)
+            other[n].start()
+            own[n].start()
 
     def dq_copies(j):
         cols = tile((core * HEADS + j) * GROUP * HEAD, GROUP * HEAD)

time: 100 us -> 100 us (level)
  no operation moved by 1% of the time
where the time goes in v5:
time: 100 us; the launch traced here: 99.9 us
  Pallas kernels  99.3 us (99%)
    pallas_call x1, Pallas kernels, body(): pl.pallas_call(kernel, out_shape=(jax.ShapeDtypeStruct(queries.shape, BF1...  97.1 us
    pallas_call x1, Pallas kernels, body(): pl.pallas_call(settle, out_shape=tuple((jax.ShapeDtypeStruct(x.shape, BF1...  2.19 us

profile of v5, /device:TPU:1, one launch (start us, length us, event | category | flops | bytes accessed | tf_op | source)
XLA Modules:
  0.0 99.9 jit_solution(9169219405250080018)
XLA Ops:
  0.6 97.1 %banded_attention_grad.1 = (bf16[128,4096]{1,0:T(8,128)(2,1)}, bf16[128,1024]{1,0:T(8,128)(2,1)}, bf16[128,1024]{1,0:T(8,128)(2,1)}) custom-call(bf16[128,4096]{1,0:T(8,128)(2,1)} %q_in.1, bf16[128,1024]{1,0:T(8,128)(2,1)} %k_in.1, bf16[128,1024]{1,0:T(8,128)(2,1)} %v_in.1, bf16[128,4096]{1,0:T(8,128)(2,1)} %o_in.1, bf16[128,4096]{1,0:T(8,128)(2,1)} %g_in.1, ...), custom_call_target="tpu_custom_call" | custom-call | tf_op jit(solution)/shard_map/banded_attention_grad/pallas_call | solution.py:435
  97.7 2.2 %settle.1 = (bf16[128,4096]{1,0:T(8,128)(2,1)}, bf16[128,1024]{1,0:T(8,128)(2,1)}, bf16[128,1024]{1,0:T(8,128)(2,1)}) custom-call(bf16[128,4096]{1,0:T(8,128)(2,1)} %get-tuple-element.6.a, bf16[128,1024]{1,0:T(8,128)(2,1)} %get-tuple-element.7.b, bf16[128,1024]{1,0:T(8,128)(2,1)} %get-tuple-element.8.c), custom_call_target="tpu_custom_call" | custom-call | tf_op jit(solution)/shard_map/settle/pallas_call | solution.py:475
